TPU v7x, 32 devices: a whole 2x2x4 slice. The times are simulated.
32 devices in a mesh: dp: 8 (over z, y), mp: 4 (over x, core).
Axes of the slice: x: 2, y: 2, z: 4, core: 2. Of those that a mesh axis runs over, the one named last changes fastest.
Arguments:
- tokens: bfloat16 [4096, 1024], P('dp'), may hold values from -6 to 6
- cotangent: bfloat16 [4096, 1024], P('dp'), may hold values from -6 to 6
- segment_ids: int32 [4096], P('dp'), may hold values from -1 to 31, as said below
- table_index: int32 [4096], P('dp'), may hold values from 0 to 1043, as said below
- group_count: int32 [8], P('dp'), may hold values from 1 to 4
- owner_list: int32 [192], replicated, may hold values from 0 to 191, each once
- step_count: int32 [1], replicated, may hold values from 2 to 20
- query_weight: bfloat16 [1024, 1024], P(None, 'mp'), may hold values from -0.1875 to 0.1875
- key_weight: bfloat16 [1024, 1024], P(None, 'mp'), may hold values from -0.1875 to 0.1875
- value_weight: bfloat16 [1024, 1024], P(None, 'mp'), may hold values from -0.1875 to 0.1875
- output_weight: bfloat16 [1024, 1024], P('mp'), may hold values from -0.5 to 0.5
- hidden_weight: bfloat16 [1024, 4096], P(None, 'mp'), may hold values from -0.1875 to 0.1875
- return_weight: bfloat16 [4096, 1024], P('mp'), may hold values from -0.09375 to 0.09375
- norm_params: float32 [4, 1024], replicated, may hold values from 0.5 to 1.5
- norm_first: float32 [4, 1024], replicated, may hold values from -0.00390625 to 0.00390625
- norm_second: float32 [4, 1024], replicated, may hold values from 7.9447e-08 to 3.17788e-07
- master_blocks: float32 [192, 4, 128, 128], P('dp', 'mp'), may hold values from -0.1875 to 0.1875
- first_moment: float32 [192, 4, 128, 128], P('dp', 'mp'), may hold values from -0.00390625 to 0.00390625
- second_moment: float32 [192, 4, 128, 128], P('dp', 'mp'), may hold values from 7.9447e-08 to 3.17788e-07
- left_vector: float32 [192, 4, 128], P('dp', 'mp'), may hold values from -6 to 6
- right_vector: float32 [192, 4, 128], P('dp', 'mp'), may hold values from -6 to 6
Outputs:
- layer_output: float32 [4096, 1024], P('dp')
- input_grad: float32 [4096, 1024], P('dp')
- block_grads: float32 [192, 4, 128, 128], P('dp', 'mp')
- block_first: float32 [192, 4, 128, 128], P('dp', 'mp')
- block_second: float32 [192, 4, 128, 128], P('dp', 'mp')
- block_master: float32 [192, 4, 128, 128], P('dp', 'mp')
- block_copy: bfloat16 [192, 4, 128, 128], P('dp', 'mp')
- norm_grads: float32 [2, 4, 1024], replicated
- norm_square: float32 [4, 1024], replicated
- norm_value: float32 [4, 1024], replicated
- clip_norm: float32 [], replicated
Inputs may be any that keep to these rules, and one draw needn't show every extreme that they name: `segment_ids`: on each dp index the items all have one length, 16, 49 or 196 patches, and lie one after another from the first slot, numbered from 0; the slots after them hold -1. Every device holds at least one item. `table_index`: rows 0 to 63 belong to images of 64 patches, 64 to 259 to images of 196, 260 to 1043 to images of 784; all slots of a dp index use the range whose image size matches its item length (64, 196, 784 patches for items of 16, 49, 196). `owner_list`: every block number appears once; slot s lies on dp index s // 24.
All inputs are finite; a program needn't handle non-finite values.
Results may differ from a plain program's by a relative error of at most 0.014.
Values may be sent and summed in bfloat16 or wider, within the bound.
No kernel may reach another device: no remote copies, remote signals or barrier semaphores. Data moves between devices by JAX's collectives and lax.ppermute only.
A program may use at most 128 MiB of HBM per device.

v0:
```python
import math

import jax
import jax.numpy as jnp
from jax import lax
from jax.sharding import PartitionSpec as P

D = 1024
HEAD = 64
BLK = 128


clip_max = 1.0
beta_one = 0.5
beta_two = 0.5
adam_eps = 1e-08
step_rate = 0.25
norm_eps = 1e-06
trust_eps = 1e-06


def position_table(table_index):
    kind = (table_index >= 64).astype(jnp.int32) + (table_index >= 260).astype(jnp.int32)
    offset = jnp.where(kind == 0, 0, jnp.where(kind == 1, 64, 260)).astype(jnp.int32)
    side = jnp.where(kind == 0, 8, jnp.where(kind == 1, 14, 28)).astype(jnp.int32)
    spacing = jnp.where(kind == 0, 1.75, jnp.where(kind == 1, 1.0, 0.5)).astype(jnp.float32)
    local_index = table_index - offset
    row_pos = (local_index // side).astype(jnp.float32) * spacing
    col_pos = (local_index % side).astype(jnp.float32) * spacing
    quarter = D // 4
    freqs = jnp.power(10000.0, -jnp.arange(quarter, dtype=jnp.float32) / quarter)
    row_arg = row_pos[:, None] * freqs[None, :]
    col_arg = col_pos[:, None] * freqs[None, :]
    return jnp.concatenate(
        [jnp.sin(row_arg), jnp.cos(row_arg), jnp.sin(col_arg), jnp.cos(col_arg)], axis=1
    )


def norm_parts(values, gain, shift):
    center = values - jnp.mean(values, axis=-1, keepdims=True)
    spread = jnp.mean(center * center, axis=-1, keepdims=True)
    inv_std = lax.rsqrt(spread + norm_eps)
    normal = center * inv_std
    return (normal * gain + shift, normal, inv_std)


def norm_back(grad_out, normal, inv_std, gain):
    scaled = grad_out * gain
    return inv_std * (
        scaled
        - jnp.mean(scaled, axis=-1, keepdims=True)
        - normal * jnp.mean(scaled * normal, axis=-1, keepdims=True)
    )


def visible(seg_query, place_query, seg_key, place_key):
    same = (seg_query[:, None] == seg_key[None, :]) & (seg_query[:, None] >= 0)
    return same | (place_query[:, None] == place_key[None, :])


def inner_rows(left, right):
    return lax.dot_general(
        left, right, (((0,), (0,)), ((), ())), preferred_element_type=jnp.float32
    )


def inner_cols(left, right):
    return lax.dot_general(
        left, right, (((1,), (1,)), ((), ())), preferred_element_type=jnp.float32
    )


def exact_gelu(values):
    return jax.nn.gelu(values, approximate=False)


def to_blocks(matrix):
    row_count, col_count = matrix.shape
    tiles = matrix.reshape(row_count // BLK, BLK, col_count // BLK, BLK)
    return tiles.transpose(0, 2, 1, 3).reshape(-1, BLK, BLK)


def masked_scores(query_block, key_heads, segment_block, place_block, segment_ids, places, scale):
    scores = (
        jnp.einsum("qhd,khd->hqk", query_block, key_heads, preferred_element_type=jnp.float32)
        * scale
    )
    allowed = visible(segment_block, place_block, segment_ids, places)
    return jnp.where(allowed[None], scores, -1e30)


def attend(query_low, key_low, value_low, segment_ids, heads, scale):
    length = query_low.shape[0]
    block_rows = min(512, length)
    blocks = length // block_rows
    key_heads = key_low.reshape(length, heads, HEAD)
    value_heads = value_low.reshape(length, heads, HEAD)
    places = jnp.arange(length, dtype=jnp.int32)

    def attend_block(pieces):
        query_block, segment_block, place_block = pieces
        scores = masked_scores(
            query_block, key_heads, segment_block, place_block, segment_ids, places, scale
        )
        peak = jnp.max(scores, axis=-1, keepdims=True)
        expon = jnp.exp(scores - peak)
        total = jnp.sum(expon, axis=-1, keepdims=True)
        probs_low = (expon / total).astype(jnp.bfloat16)
        mixed_block = jnp.einsum(
            "hqk,khd->qhd", probs_low, value_heads, preferred_element_type=jnp.float32
        )
        return (mixed_block, (peak + jnp.log(total))[..., 0])

    mixed, log_total = lax.map(
        attend_block,
        (
            query_low.reshape(blocks, block_rows, heads, HEAD),
            segment_ids.reshape(blocks, block_rows),
            places.reshape(blocks, block_rows),
        ),
    )
    return (mixed.reshape(length, heads * HEAD), log_total)


def attend_back(query_low, key_low, value_low, segment_ids, log_total, grad_mixed, heads, scale):
    length = query_low.shape[0]
    block_rows = min(512, length)
    blocks = length // block_rows
    key_heads = key_low.reshape(length, heads, HEAD)
    value_heads = value_low.reshape(length, heads, HEAD)
    places = jnp.arange(length, dtype=jnp.int32)

    def back_block(carry, pieces):
        grad_keys, grad_values = carry
        query_block, segment_block, place_block, total_block, grad_block = pieces
        scores = masked_scores(
            query_block, key_heads, segment_block, place_block, segment_ids, places, scale
        )
        probs = jnp.exp(scores - total_block[:, :, None])
        probs_low = probs.astype(jnp.bfloat16)
        grad_values = grad_values + jnp.einsum(
            "hqk,qhd->khd", probs_low, grad_block, preferred_element_type=jnp.float32
        )
        grad_probs = jnp.einsum(
            "qhd,khd->hqk", grad_block, value_heads, preferred_element_type=jnp.float32
        )
        grad_scores = probs * (grad_probs - jnp.sum(probs * grad_probs, axis=-1, keepdims=True))
        scores_low = grad_scores.astype(jnp.bfloat16)
        grad_query = (
            jnp.einsum("hqk,khd->qhd", scores_low, key_heads, preferred_element_type=jnp.float32)
            * scale
        )
        grad_keys = (
            grad_keys
            + jnp.einsum(
                "hqk,qhd->khd", scores_low, query_block, preferred_element_type=jnp.float32
            )
            * scale
        )
        return ((grad_keys, grad_values), grad_query)

    zeros_kv = jnp.zeros((length, heads, HEAD), jnp.float32)
    (grad_keys, grad_values), grad_queries = lax.scan(
        back_block,
        (zeros_kv, zeros_kv),
        (
            query_low.reshape(blocks, block_rows, heads, HEAD),
            segment_ids.reshape(blocks, block_rows),
            places.reshape(blocks, block_rows),
            log_total,
            grad_mixed.reshape(blocks, block_rows, heads, HEAD),
        ),
    )
    width = heads * HEAD
    return (
        grad_queries.reshape(length, width),
        grad_keys.reshape(length, width),
        grad_values.reshape(length, width),
    )


def reflect_left(matrix, vector):
    coef = 2.0 / jnp.sum(vector * vector, axis=-1)
    proj = jnp.einsum("sr,src->sc", vector, matrix, precision=lax.Precision.HIGHEST)
    return matrix - coef[:, None, None] * vector[:, :, None] * proj[:, None, :]


def reflect_right(matrix, vector):
    coef = 2.0 / jnp.sum(vector * vector, axis=-1)
    proj = jnp.einsum("src,sc->sr", matrix, vector, precision=lax.Precision.HIGHEST)
    return matrix - coef[:, None, None] * proj[:, :, None] * vector[:, None, :]


def shards(
    tokens,
    cotangent,
    segment_ids,
    table_index,
    group_count,
    owner_list,
    step_count,
    query_weight,
    key_weight,
    value_weight,
    output_weight,
    hidden_weight,
    return_weight,
    norm_params,
    norm_first,
    norm_second,
    master_blocks,
    first_moment,
    second_moment,
    left_vector,
    right_vector,
):
    heads = query_weight.shape[1] // HEAD
    scale = 1.0 / math.sqrt(HEAD)
    layer_in = tokens.astype(jnp.float32) + position_table(table_index)
    valid_row = (segment_ids >= 0).astype(jnp.float32)
    normed, first_hat, first_inv = norm_parts(layer_in, norm_params[0], norm_params[1])
    normed_low = normed.astype(jnp.bfloat16)
    query_low = jnp.dot(normed_low, query_weight, preferred_element_type=jnp.float32).astype(
        jnp.bfloat16
    )
    key_low = jnp.dot(normed_low, key_weight, preferred_element_type=jnp.float32).astype(
        jnp.bfloat16
    )
    value_low = jnp.dot(normed_low, value_weight, preferred_element_type=jnp.float32).astype(
        jnp.bfloat16
    )
    mixed, log_total = attend(query_low, key_low, value_low, segment_ids, heads, scale)
    mixed_low = mixed.astype(jnp.bfloat16)
    attn = lax.psum(
        jnp.dot(mixed_low, output_weight, preferred_element_type=jnp.float32).astype(jnp.bfloat16),
        "mp",
    ).astype(jnp.float32)
    hidden_in = layer_in + attn
    second, second_hat, second_inv = norm_parts(hidden_in, norm_params[2], norm_params[3])
    second_low = second.astype(jnp.bfloat16)
    pre_act = jnp.dot(second_low, hidden_weight, preferred_element_type=jnp.float32)
    act_value, gelu_back = jax.vjp(exact_gelu, pre_act)
    act_low = act_value.astype(jnp.bfloat16)
    mlp = lax.psum(
        jnp.dot(act_low, return_weight, preferred_element_type=jnp.float32).astype(jnp.bfloat16),
        "mp",
    ).astype(jnp.float32)
    layer_output = hidden_in + mlp
    grad_out = cotangent.astype(jnp.float32) * valid_row[:, None]
    grad_out_low = grad_out.astype(jnp.bfloat16)
    grad_return = inner_rows(act_low, grad_out_low)
    grad_act = inner_cols(grad_out_low, return_weight)
    grad_pre_low = gelu_back(grad_act)[0].astype(jnp.bfloat16)
    grad_hidden = inner_rows(second_low, grad_pre_low)
    grad_second = lax.psum(
        inner_cols(grad_pre_low, hidden_weight).astype(jnp.bfloat16), "mp"
    ).astype(jnp.float32)
    grad_hid = grad_out + norm_back(grad_second, second_hat, second_inv, norm_params[2])
    grad_attn_low = grad_hid.astype(jnp.bfloat16)
    grad_output = inner_rows(mixed_low, grad_attn_low)
    grad_mixed_low = inner_cols(grad_attn_low, output_weight).astype(jnp.bfloat16)
    grad_queries, grad_keys, grad_values = attend_back(
        query_low, key_low, value_low, segment_ids, log_total, grad_mixed_low, heads, scale
    )
    gq_low = grad_queries.astype(jnp.bfloat16)
    gk_low = grad_keys.astype(jnp.bfloat16)
    gv_low = grad_values.astype(jnp.bfloat16)
    grad_query = inner_rows(normed_low, gq_low)
    grad_key = inner_rows(normed_low, gk_low)
    grad_value = inner_rows(normed_low, gv_low)
    normed_part = (
        inner_cols(gq_low, query_weight)
        + inner_cols(gk_low, key_weight)
        + inner_cols(gv_low, value_weight)
    )
    grad_normed = lax.psum(normed_part.astype(jnp.bfloat16), "mp").astype(jnp.float32)
    input_grad = grad_hid + norm_back(grad_normed, first_hat, first_inv, norm_params[0])
    norm_grads = jnp.stack(
        [
            jnp.sum(grad_normed * first_hat, axis=0),
            jnp.sum(grad_normed, axis=0),
            jnp.sum(grad_second * second_hat, axis=0),
            jnp.sum(grad_second, axis=0),
        ],
        axis=0,
    )
    weight = group_count.astype(jnp.float32)[0]
    local_blocks = (
        jnp.concatenate(
            [
                to_blocks(grad_query),
                to_blocks(grad_key),
                to_blocks(grad_value),
                to_blocks(grad_output),
                to_blocks(grad_hidden),
                to_blocks(grad_return),
            ],
            axis=0,
        )
        * weight
    )
    ordered = jnp.take(local_blocks, owner_list, axis=0)
    slot_count = master_blocks.shape[0]
    summed = lax.psum(ordered, "dp")
    owned = lax.dynamic_slice_in_dim(summed, lax.axis_index("dp") * slot_count, slot_count, 0)
    norm_total, count_total = lax.psum((norm_grads * weight, weight), "dp")
    owned = owned / count_total
    norm_grad = norm_total / count_total
    leader = (lax.axis_index("dp") == 0) & (lax.axis_index("mp") == 0)
    partial_sq = jnp.sum(owned * owned) + jnp.where(leader, jnp.sum(norm_grad * norm_grad), 0.0)
    total_sq = lax.psum(partial_sq, ("dp", "mp"))
    clip_norm = jnp.sqrt(total_sq)
    factor = jnp.minimum(1.0, clip_max / clip_norm)
    clipped = owned * factor
    norm_clipped = norm_grad * factor
    step_value = step_count[0].astype(jnp.float32)
    corr_one = 1.0 - jnp.power(beta_one, step_value)
    corr_two = 1.0 - jnp.power(beta_two, step_value)
    left_vec = left_vector.reshape(slot_count, BLK)
    right_vec = right_vector.reshape(slot_count, BLK)
    old_first = first_moment.reshape(slot_count, BLK, BLK)
    old_second = second_moment.reshape(slot_count, BLK, BLK)
    old_master = master_blocks.reshape(slot_count, BLK, BLK)
    rotated = reflect_right(reflect_left(clipped, left_vec), right_vec)
    new_first = beta_one * old_first + (1.0 - beta_one) * rotated
    new_second = beta_two * old_second + (1.0 - beta_two) * rotated * rotated
    normal_step = new_first / corr_one / (jnp.sqrt(new_second / corr_two) + adam_eps)
    turned = reflect_right(reflect_left(normal_step, left_vec), right_vec)
    trust = jnp.sqrt(jnp.mean(old_master * old_master, axis=(1, 2)) + trust_eps) / jnp.sqrt(
        jnp.mean(turned * turned, axis=(1, 2)) + trust_eps
    )
    new_master = old_master - step_rate * trust[:, None, None] * turned
    norm_m = beta_one * norm_first + (1.0 - beta_one) * norm_clipped
    norm_v = beta_two * norm_second + (1.0 - beta_two) * norm_clipped * norm_clipped
    norm_new = norm_params - step_rate * (norm_m / corr_one) / (
        jnp.sqrt(norm_v / corr_two) + adam_eps
    )
    norm_pair = jnp.stack([norm_clipped, norm_m], axis=0)
    shard_shape = (slot_count, 1, BLK, BLK)
    return (
        layer_output,
        input_grad,
        clipped.reshape(shard_shape),
        new_first.reshape(shard_shape),
        new_second.reshape(shard_shape),
        new_master.reshape(shard_shape),
        new_master.astype(jnp.bfloat16).reshape(shard_shape),
        norm_pair,
        norm_v,
        norm_new,
        clip_norm,
    )


def solution(mesh):
    placed = (
        P("dp", None),
        P("dp", None),
        P("dp"),
        P("dp"),
        P("dp"),
        P(),
        P(),
        P(None, "mp"),
        P(None, "mp"),
        P(None, "mp"),
        P("mp", None),
        P(None, "mp"),
        P("mp", None),
        P(),
        P(),
        P(),
        P("dp", "mp", None, None),
        P("dp", "mp", None, None),
        P("dp", "mp", None, None),
        P("dp", "mp", None),
        P("dp", "mp", None),
    )
    return jax.shard_map(
        shards,
        mesh=mesh,
        in_specs=placed,
        out_specs=(
            P("dp", None),
            P("dp", None),
            P("dp", "mp", None, None),
            P("dp", "mp", None, None),
            P("dp", "mp", None, None),
            P("dp", "mp", None, None),
            P("dp", "mp", None, None),
            P(),
            P(),
            P(),
            P(),
        ),
        check_vma=False,
    )
```

profile of v0, /device:TPU:0, one launch (start us, length us, event | category | flops | bytes accessed | tf_op | source)
XLA Modules:
  0.0 673.4 jit_solution(4944864439973134867)
XLA Ops:
  9.2 3.7 multiply_sine_fusion.1
  28.9 32.8 %all-reduce.7.cloned.1.call-done = bf16[512,1024]{1,0:T(8,128)(2,1)} async-done(((bf16[512,1024]{1,0:T(8,128)(2,1)}), bf16[512,1024]{1,0:T(8,128)(2,1)}) %all-reduce.7.cloned.1.call-update) | async-done | bytes 1048592 | tf_op jit(solution)/shard_map/psum | solution.py:234
  64.3 6.8 %multiply_convert_fusion.1 = (bf16[512,1024]{1,0:T(8,128)(2,1)}, f32[512,1024]{1,0:T(8,128)S(1)}, f32[512,1024]{1,0:T(8,128)S(1)}) fusion(bf16[1024,1024]{1,0:T(8,128)(2,1)S(1)} %copy-done, f32[512,1024]{1,0:T(8,128)S(1)} %get-tuple-element.112, f32[1024]{0:T(1024)S(1)} %bitcast.273, f32[1024]{0:T(1024)S(1)} %bitcast.260, f32[512]{0:T(512)S(1)} %add_rsqrt_fusion, ...), kind=kOutput, calls=%fused_computation.47 | convolution fusion | flops 1110441984 | bytes 9449472 | tf_op jit(solution)/shard_map/dot_general | solution.py:241
  73.9 2.3 convolution_convert_fusion
  76.1 5.4 convolution_bitcast_fusion.1
  85.0 2.7 copy.50
  88.7 2.7 copy.51
  93.7 24.5 %all-reduce.9.cloned.1.call-done = bf16[512,1024]{1,0:T(8,128)(2,1)} async-done(((bf16[512,1024]{1,0:T(8,128)(2,1)}), bf16[512,1024]{1,0:T(8,128)(2,1)}) %all-reduce.9.cloned.1.call-update) | async-done | bytes 1048592 | tf_op jit(solution)/shard_map/psum | solution.py:255
  118.2 2.3 fusion.17
  137.0 3.2 add_convert_fusion
  146.3 2.4 constant_dynamic-update-slice_fusion.1
  152.2 11.9 %broadcast_multiply_fusion = f32[192,128,128]{2,1,0:T(8,128)} fusion(f32[192,128,128]{2,1,0:T(8,128)} %constant_dynamic-update-slice_fusion, f32[]{:T(128)} %bitcast.52), kind=kLoop, calls=%fused_computation.2 | loop fusion | flops 3145728 | bytes 25165828 | tf_op jit(solution)/shard_map/mul | solution.py:289
  164.1 15.4 %gather_fusion = f32[192,128,128]{2,1,0:T(8,128)} fusion(f32[192,128,128]{2,1,0:T(8,128)} %broadcast_multiply_fusion, s32[1024]{0:T(1024)S(1)} %pad_clamp_fusion), kind=kCustom, calls=%fused_computation | custom fusion | bytes 25166592 | tf_op jit(solution)/shard_map/jit(_take)/gather | solution.py:302
  179.5 10.1 %broadcast_select_fusion = f32[192,128,128]{2,1,0:T(8,128)} fusion(f32[192,128,128]{2,1,0:T(8,128)} %gather_fusion, pred[192]{0:T(512)(128)(4,1)S(1)} %compare_and_fusion), kind=kLoop, calls=%fused_computation.1 | loop fusion | flops 3145728 | bytes 25166016 | tf_op jit(solution)/shard_map/jit(_take)/select_n | solution.py:302
  194.7 41.2 %all-reduce = (f32[]{:T(128)}, f32[4,1024]{1,0:T(4,128)S(1)}) all-reduce(f32[]{:T(128)} %bitcast.52, f32[4,1024]{1,0:T(4,128)S(1)} %maximum_multiply_fusion), channel_id=1, replica_groups=mesh['dp'=8,'mp'=4] {'dp'}, use_global_device_ids=true, to_apply=%region_16.17 | all-reduce | flops 4097 | bytes 32776 | tf_op jit(solution)/shard_map/psum | solution.py:306
  238.0 3.6 fusion.10
  241.6 353.4 %all-reduce.11.cloned.1.call-done = f32[192,128,128]{2,1,0:T(8,128)} async-done(((f32[192,128,128]{2,1,0:T(8,128)}), f32[192,128,128]{2,1,0:T(8,128)}) %all-reduce.11.cloned.1.call-update) | async-done | bytes 12582928 | tf_op jit(solution)/shard_map/psum | solution.py:304
  595.0 3.1 multiply_reduce_fusion.4
  598.8 3.4 convert_add_fusion
  602.1 39.3 %psum.63 = f32[]{:T(128)} all-reduce(f32[]{:T(128)S(6)} %add.172), channel_id=1, replica_groups=mesh['dp'=8,'mp'=4] {'dp','mp'}, use_global_device_ids=true, to_apply=%region_24.25 | all-reduce | flops 1 | bytes 8 | tf_op jit(solution)/shard_map/psum | solution.py:311
  642.1 3.6 fusion.34
  645.8 5.1 fusion.31
  650.9 4.8 multiply_divide_fusion
  657.2 2.6 fusion.32
  (179 shorter events, 67.5 us)
Async XLA Ops:
  7.2 57.0 %copy-start = (bf16[1024,1024]{1,0:T(8,128)(2,1)S(1)}, bf16[1024,1024]{1,0:T(8,128)(2,1)}, u32[]{:S(2)}) copy-start(bf16[1024,1024]{1,0:T(8,128)(2,1)} %param.32) | copy-start | bytes 6291460
  7.2 5.7 copy-start.28
  7.2 54.5 %all-reduce.7.cloned.1.call-start = ((), (), s32[]{:S(2)}) async-start(), calls=%async_computation | async-start | bytes 2097152 | tf_op jit(solution)/shard_map/psum | solution.py:234
  15.5 2.9 copy-start.32
  22.7 95.5 %all-reduce.9.cloned.1.call-start = ((), (), s32[]{:S(2)}) async-start(), calls=%async_computation.1 | async-start | bytes 2097152 | tf_op jit(solution)/shard_map/psum | solution.py:255
  26.0 2.9 copy-start.43
  63.8 7.2 %copy-start.6 = (f32[512,1024]{1,0:T(8,128)}, f32[512,1024]{1,0:T(8,128)S(1)}, u32[]{:S(2)}) copy-start(f32[512,1024]{1,0:T(8,128)S(1)} %get-tuple-element.112) | copy-start | bytes 6291460
  64.2 6.8 %copy-start.34 = (bf16[512,1024]{1,0:T(8,128)(2,1)S(1)}, bf16[512,1024]{1,0:T(8,128)(2,1)}, u32[]{:S(2)}) copy-start(bf16[512,1024]{1,0:T(8,128)(2,1)} %param.22) | copy-start | bytes 3145732
  64.2 6.8 %copy-start.44 = (bf16[1024,1024]{1,0:T(8,128)(2,1)S(1)}, bf16[1024,1024]{1,0:T(8,128)(2,1)}, u32[]{:S(2)}) copy-start(bf16[1024,1024]{1,0:T(8,128)(2,1)} %param.33) | copy-start | bytes 6291460
  76.1 5.7 copy-start.35
  76.1 5.7 copy-start.46
  81.6 110.9 %all-reduce.13.cloned.1.call-start = ((), (), s32[]{:S(2)}) async-start(), calls=%async_computation.3 | async-start | bytes 4194304 | tf_op jit(solution)/shard_map/psum | solution.py:244
  88.7 2.7 copy-start.45
  91.5 26.8 %copy-start.7 = (f32[512,1024]{1,0:T(8,128)S(1)}, f32[512,1024]{1,0:T(8,128)}, u32[]{:S(2)}) copy-start(f32[512,1024]{1,0:T(8,128)} %copy-done.6) | copy-start | bytes 6291460
  120.6 2.7 copy-start.3
  140.3 454.7 %all-reduce.11.cloned.1.call-start = ((), (), s32[]{:S(2)}) async-start(), calls=%async_computation.2 | async-start | bytes 25165824 | tf_op jit(solution)/shard_map/psum | solution.py:304
  146.3 3.7 copy-start.10
  189.5 2.9 copy-start.5
  192.4 45.5 %copy-start.15 = (bf16[512,1024]{1,0:T(8,128)(2,1)S(1)}, bf16[512,1024]{1,0:T(8,128)(2,1)}, u32[]{:S(2)}) copy-start(bf16[512,1024]{1,0:T(8,128)(2,1)} %get-tuple-element.102) | copy-start | bytes 3145732
  241.6 357.2 %copy-start.29 = (bf16[512,1024]{1,0:T(8,128)(2,1)S(1)}, bf16[512,1024]{1,0:T(8,128)(2,1)}, u32[]{:S(2)}) copy-start(bf16[512,1024]{1,0:T(8,128)(2,1)} %get-tuple-element.101) | copy-start | bytes 3145732
  645.8 5.1 copy-start.26
  645.8 5.1 copy-start.27
  655.7 5.4 copy-start.11
  661.1 4.2 copy-start.1
  (29 other events, 48.3 us)
Sparse Core Ops, SparseCore 0:
  22.9 38.8 all-reduce.6
  81.7 36.4 all-reduce.8
  140.4 51.9 all-reduce.12
  196.9 398.0 all-reduce.10
where the time goes:
time: 681 us; the launch traced here: 673 us
  waiting for transfers between devices  411 us (60%)
  blocking collectives  80.5 us (12%)
  other arithmetic  64.5 us (9%)
  matrix products  50.2 us (7%)
  local copies, waits for them, and re-layouts  47.1 us (7%)
  between operations  19.5 us (3%)
    psum x1, waiting for transfers between devices, shards(): summed = lax.psum(ordered, 'dp')  353 us
    psum x1, blocking collectives, shards(): norm_total, count_total = lax.psum((norm_grads * weight, weight), 'dp')  41.2 us
    psum x1, blocking collectives, shards(): total_sq = lax.psum(partial_sq, ('dp', 'mp'))  39.3 us
    psum x1, waiting for transfers between devices, shards(): lax.psum(jnp.dot(mixed_low, output_weight, preferred_element_type=jnp.flo...  32.8 us
    psum x1, waiting for transfers between devices, shards(): lax.psum(inner_cols(grad_pre_low, hidden_weight).astype(jnp.bfloat16), 'mp')  24.5 us
    unnamed x106, local copies, waits for them, and re-layouts  20.1 us
    gather x1, local copies, waits for them, and re-layouts, shards(): ordered = jnp.take(local_blocks, owner_list, axis=0)  15.4 us
  transfers between devices with their start and end apart: 4, of which 3 were waited for; matrix products, arithmetic and copies ran while one was open for 11% of the time, Pallas kernels for 0%

commit v1 on v0

v1 whole, which is shorter than its diff:
```python
import functools
import math

import jax
import jax.numpy as jnp
import numpy as np
from jax import lax
from jax.experimental import pallas as pl
from jax.experimental.pallas import tpu as pltpu
from jax.sharding import PartitionSpec as P

D = 1024
HEAD = 64
BLK = 128
LANES = 128
POS_ROWS = 64
SEG_ROWS = 32

clip_max = 1.0
beta_one = 0.5
beta_two = 0.5
adam_eps = 1e-08
step_rate = 0.25
norm_eps = 1e-06
trust_eps = 1e-06

F32 = jnp.float32
BF16 = jnp.bfloat16
VMEM_LIMIT = 48 * 1024 * 1024

ERF_P = 0.425
ERF_COEF = (
    0.11983931305209315,
    0.12092032287702306,
    0.10035292560006456,
    0.12754356284084392,
    -0.051626023300101125,
    0.20380940869554587,
    -0.1565787944569494,
    0.035739213095996265,
)


def position_rows():
    coords = np.concatenate(
        [1.75 * np.arange(8), 1.0 * np.arange(14), 0.5 * np.arange(28), np.zeros(POS_ROWS - 50)]
    )
    quarter = D // 4
    freqs = np.power(np.float32(10000.0), -np.arange(quarter, dtype=np.float32) / np.float32(quarter))
    args = (coords.astype(np.float32)[:, None] * freqs.astype(np.float32)[None, :]).astype(np.float64)
    table = np.concatenate([np.sin(args), np.cos(args)], axis=1).astype(np.float32)
    parts = []
    rest = table
    for _ in range(3):
        part = rest.astype(jnp.bfloat16)
        parts.append(part)
        rest = rest - part.astype(np.float32)
    return np.concatenate(parts, axis=0)


def dot_nn(left, right):
    return lax.dot_general(left, right, (((1,), (0,)), ((), ())), preferred_element_type=F32)


def dot_nt(left, right):
    return lax.dot_general(left, right, (((1,), (1,)), ((), ())), preferred_element_type=F32)


def dot_tn(left, right):
    return lax.dot_general(left, right, (((0,), (0,)), ((), ())), preferred_element_type=F32)


def norm_hat(values):
    center = values - jnp.mean(values, axis=-1, keepdims=True)
    inv_std = lax.rsqrt(jnp.mean(center * center, axis=-1, keepdims=True) + norm_eps)
    return (center * inv_std, inv_std)


def norm_back(grad_out, normal, inv_std, gain):
    scaled = grad_out * gain
    return inv_std * (
        scaled
        - jnp.mean(scaled, axis=-1, keepdims=True)
        - normal * jnp.mean(scaled * normal, axis=-1, keepdims=True)
    )


def gelu_parts(values):
    bell = jnp.exp(-0.5 * values * values)
    t = 1.0 / (1.0 + (ERF_P / math.sqrt(2.0)) * jnp.abs(values))
    poly = ERF_COEF[-1]
    for coef in ERF_COEF[-2::-1]:
        poly = poly * t + coef
    tail = poly * t * bell
    dist = jnp.where(values >= 0.0, 1.0 - tail, tail)
    return (values * dist, dist + values * ((1.0 / math.sqrt(2.0 * math.pi)) * bell))


def item_rows(seg_row):
    rows = lax.broadcasted_iota(jnp.int32, (SEG_ROWS, seg_row.shape[1]), 0)
    return jnp.where(rows == seg_row, 1.0, 0.0).astype(BF16)


def head_lanes(rows, head):
    lanes = lax.broadcasted_iota(jnp.int32, (rows, LANES), 1)
    return (lanes < HEAD) if head == 0 else (lanes >= HEAD)


def forward_kernel(
    me_ref,
    tok_ref,
    index_ref,
    seg_ref,
    table_ref,
    norm_ref,
    wq_ref,
    wk_ref,
    wv_ref,
    wo_ref,
    layer_ref,
    normed_ref,
    q_ref,
    k_ref,
    v_ref,
    mixed_ref,
    lse_ref,
    bias_ref,
    keep_ref,
    send_ref,
    part_ref,
):
    length = tok_ref.shape[0]
    index = index_ref[...]
    big = index >= 260
    mid = index >= 64
    offset = jnp.where(big, 260, jnp.where(mid, 64, 0))
    base = jnp.where(big, 22, jnp.where(mid, 8, 0))
    side = jnp.where(big, 28, jnp.where(mid, 14, 8))
    local = index - offset
    inv_side = jnp.where(big, 1.0 / 28.0, jnp.where(mid, 1.0 / 14.0, 1.0 / 8.0)).astype(F32)
    row = jnp.floor((local.astype(F32) + 0.5) * inv_side).astype(jnp.int32)
    col = local - row * side
    rows_iota = lax.broadcasted_iota(jnp.int32, (3 * POS_ROWS, length), 0)
    rows_iota = rows_iota & (POS_ROWS - 1)
    row_hot = jnp.where(rows_iota == base + row, 1.0, 0.0).astype(BF16)
    col_hot = jnp.where(rows_iota == base + col, 1.0, 0.0).astype(BF16)
    table = table_ref[...]
    items = item_rows(seg_ref[...])
    same = dot_tn(items, items)
    diag = lax.broadcasted_iota(jnp.int32, (length, length), 0) == lax.broadcasted_iota(
        jnp.int32, (length, length), 1
    )
    bias_ref[...] = jnp.where((same > 0.5) | diag, 0.0, -1e30)
    half = D // 2
    layer_ref[:, :half] = dot_tn(row_hot, table) + tok_ref[:, :half].astype(F32)
    layer_ref[:, half:] = dot_tn(col_hot, table) + tok_ref[:, half:].astype(F32)
    step = 128
    for at in range(0, length, step):
        rows = slice(at, at + step)
        hat, _ = norm_hat(layer_ref[rows, :])
        normed_ref[rows, :] = (hat * norm_ref[0:1, :] + norm_ref[1:2, :]).astype(BF16)
    normed = normed_ref[...]
    q_ref[...] = dot_nn(normed, wq_ref[...]).astype(BF16)
    k_ref[...] = dot_nn(normed, wk_ref[...]).astype(BF16)
    v_ref[...] = dot_nn(normed, wv_ref[...]).astype(BF16)
    scale = 1.0 / math.sqrt(HEAD)
    for pair in range(q_ref.shape[1] // LANES):
        cols = slice(pair * LANES, (pair + 1) * LANES)
        keys = k_ref[:, cols]
        vals = v_ref[:, cols]
        for at in range(0, length, step):
            rows = slice(at, at + step)
            query = q_ref[rows, cols] * scale
            outs = []
            for head in range(2):
                here = head_lanes(step, head)
                scores = dot_nt(jnp.where(here, query, 0.0).astype(BF16), keys) + bias_ref[rows, :]
                peak = jnp.max(scores, axis=-1, keepdims=True)
                expon = jnp.exp(scores - peak)
                total = jnp.sum(expon, axis=-1, keepdims=True)
                outs.append(dot_nn(expon.astype(BF16), vals) * (1.0 / total))
                number = pair * 2 + head
                lse_ref[rows, number : number + 1] = peak + jnp.log(total)
            mixed_ref[rows, cols] = jnp.where(head_lanes(step, 0), outs[0], outs[1]).astype(BF16)
    part_ref[...] = dot_nn(mixed_ref[...], wo_ref[...]).astype(BF16)
    split_halves(me_ref, part_ref, keep_ref, send_ref)


def split_halves(me_ref, part_ref, keep_ref, send_ref):
    half = keep_ref.shape[0]
    bit = me_ref[1] & 1
    keep_ref[...] = part_ref[pl.ds(pl.multiple_of(bit * half, half), half), :]
    send_ref[...] = part_ref[pl.ds(pl.multiple_of((1 - bit) * half, half), half), :]


def grad_out_kernel(cot_ref, seg_ref, wr_ref, gout_ref, gact_ref):
    items = item_rows(seg_ref[...])
    valid = dot_tn(items, jnp.ones((SEG_ROWS, LANES), BF16))
    for at in range(0, D, LANES):
        cols = slice(at, at + LANES)
        gout_ref[:, cols] = (cot_ref[:, cols].astype(F32) * valid).astype(BF16)
    gact_ref[...] = dot_nt(gout_ref[...], wr_ref[...])


def feed_kernel(
    me_ref,
    own_ref,
    other_ref,
    layer_ref,
    norm_ref,
    wh_ref,
    gact_ref,
    hid_ref,
    second_ref,
    act_ref,
    gpre_ref,
    keep_ref,
    send_ref,
    pre_ref,
):
    half = own_ref.shape[0]
    bit = me_ref[1] & 1
    step = 64
    for part_ref, which, out_ref in ((other_ref, 1 - bit, send_ref), (own_ref, bit, keep_ref)):
        start = pl.multiple_of(which * half, half)

        @pl.loop(0, half // step)
        def _(i, part_ref=part_ref, start=start):
            at = pl.multiple_of(i * step, step)
            rows = pl.ds(pl.multiple_of(start + at, step), step)
            hid = layer_ref[rows, :] + part_ref[pl.ds(at, step), :].astype(F32)
            hid_ref[rows, :] = hid
            hat, _ = norm_hat(hid)
            second_ref[rows, :] = (hat * norm_ref[2:3, :] + norm_ref[3:4, :]).astype(BF16)

        rows = pl.ds(start, half)
        pre_ref[...] = dot_nn(second_ref[rows, :], wh_ref[...])

        @pl.loop(0, half // 32)
        def _(i, start=start):
            at = pl.multiple_of(i * 32, 32)
            rows = pl.ds(pl.multiple_of(start + at, 32), 32)
            act, slope = gelu_parts(pre_ref[pl.ds(at, 32), :])
            act_ref[rows, :] = act.astype(BF16)
            gpre_ref[rows, :] = (gact_ref[rows, :] * slope).astype(BF16)

        out_ref[...] = dot_nt(gpre_ref[rows, :], wh_ref[...]).astype(BF16)


def store_blocks(nat_ref, base, left_ref, right_ref, weight):
    width = right_ref.shape[1]
    across = width // BLK
    wide = 256
    left = left_ref[...]
    for at in range(0, width, wide):
        grad = (dot_tn(left, right_ref[:, at : at + wide]) * weight).astype(BF16)
        for i in range(left_ref.shape[1] // BLK):
            for j in range(wide // BLK):
                nat_ref[base + i * across + at // BLK + j] = grad[
                    i * BLK : (i + 1) * BLK, j * BLK : (j + 1) * BLK
                ]


def feed_grad_kernel(
    me_ref,
    scal_ref,
    act_ref,
    gout_ref,
    second_ref,
    gpre_ref,
    wr_ref,
    nat_ref,
    keep_ref,
    send_ref,
    part_ref,
):
    weight = scal_ref[0]
    store_blocks(nat_ref, 0, second_ref, gpre_ref, weight)
    store_blocks(nat_ref, 64, act_ref, gout_ref, weight)
    part_ref[...] = dot_nn(act_ref[...], wr_ref[...]).astype(BF16)
    split_halves(me_ref, part_ref, keep_ref, send_ref)


def bit_reverse(value, bits):
    out = 0
    for i in range(bits):
        out |= ((value >> i) & 1) << (bits - 1 - i)
    return out


def backward_kernel(
    chunks,
    n_dp,
    me_ref,
    owner_ref,
    scal_ref,
    own_ref,
    other_ref,
    hid_ref,
    gout_ref,
    norm_ref,
    normed_ref,
    q_ref,
    k_ref,
    v_ref,
    mixed_ref,
    lse_ref,
    bias_ref,
    wo_ref,
    early_ref,
    *rest,
):
    ghid_ref, gq_ref, gk_ref, gv_ref = rest[:4]
    chunk_refs = rest[4 : 4 + 2 * len(chunks)]
    gattn_ref, gmix_ref, late_ref = rest[4 + 2 * len(chunks) :]
    half = own_ref.shape[0]
    length = 2 * half
    bit = me_ref[1] & 1
    weight = scal_ref[0]
    step = 64
    for part_ref, which in ((other_ref, 1 - bit), (own_ref, bit)):
        start = pl.multiple_of(which * half, half)

        @pl.loop(0, half // step)
        def _(i, part_ref=part_ref, start=start):
            at = pl.multiple_of(i * step, step)
            rows = pl.ds(pl.multiple_of(start + at, step), step)
            hat, inv_std = norm_hat(hid_ref[rows, :])
            grad = part_ref[pl.ds(at, step), :].astype(F32)
            ghid = gout_ref[rows, :].astype(F32) + norm_back(grad, hat, inv_std, norm_ref[2:3, :])
            ghid_ref[rows, :] = ghid
            gattn_ref[rows, :] = ghid.astype(BF16)

    gmix_ref[...] = dot_nt(gattn_ref[...], wo_ref[...]).astype(BF16)
    scale = 1.0 / math.sqrt(HEAD)
    step = 128
    for pair in range(q_ref.shape[1] // LANES):
        cols = slice(pair * LANES, (pair + 1) * LANES)
        keys = k_ref[:, cols]
        vals = v_ref[:, cols]
        grad_keys = [None, None]
        grad_vals = [None, None]
        for at in range(0, length, step):
            rows = slice(at, at + step)
            query = q_ref[rows, cols] * scale
            gmix = gmix_ref[rows, cols]
            grad_query = []
            for head in range(2):
                here = head_lanes(step, head)
                number = pair * 2 + head
                scores = dot_nt(jnp.where(here, query, 0.0).astype(BF16), keys) + bias_ref[rows, :]
                probs = jnp.exp(scores - lse_ref[rows, number : number + 1])
                grad_probs = dot_nt(jnp.where(here, gmix, 0.0).astype(BF16), vals)
                grad_scores = (
                    probs * (grad_probs - jnp.sum(probs * grad_probs, axis=-1, keepdims=True))
                ).astype(BF16)
                gv = dot_tn(probs.astype(BF16), gmix)
                gk = dot_tn(grad_scores, query)
                grad_vals[head] = gv if at == 0 else grad_vals[head] + gv
                grad_keys[head] = gk if at == 0 else grad_keys[head] + gk
                grad_query.append(dot_nn(grad_scores, keys))
            first = head_lanes(step, 0)
            gq_ref[rows, cols] = (jnp.where(first, grad_query[0], grad_query[1]) * scale).astype(
                BF16
            )
        first = head_lanes(length, 0)
        gk_ref[:, cols] = jnp.where(first, grad_keys[0], grad_keys[1]).astype(BF16)
        gv_ref[:, cols] = jnp.where(first, grad_vals[0], grad_vals[1]).astype(BF16)
    store_blocks(late_ref, 0, normed_ref, gq_ref, weight)
    store_blocks(late_ref, 16, normed_ref, gk_ref, weight)
    store_blocks(late_ref, 32, normed_ref, gv_ref, weight)
    store_blocks(late_ref, 48, mixed_ref, gattn_ref, weight)
    slots = sum(chunks)
    bits = n_dp.bit_length() - 1
    offset = 0
    for number, count in enumerate(chunks):
        for order in range(n_dp):
            dest = me_ref[0] ^ bit_reverse(order, bits)
            out_ref = chunk_refs[2 * number + (0 if order < n_dp // 2 else 1)]
            at = (order % (n_dp // 2)) * count
            for j in range(count):
                block = owner_ref[dest * slots + offset + j]
                out_ref[at + j] = jnp.where(
                    block < late_ref.shape[0],
                    late_ref[jnp.minimum(block, late_ref.shape[0] - 1)],
                    early_ref[jnp.maximum(block - late_ref.shape[0], 0)],
                )
        offset += count


def normed_grad_kernel(
    me_ref, gq_ref, gk_ref, gv_ref, wq_ref, wk_ref, wv_ref, keep_ref, send_ref, part_ref
):
    part_ref[...] = (
        dot_nt(gq_ref[...], wq_ref[...])
        + dot_nt(gk_ref[...], wk_ref[...])
        + dot_nt(gv_ref[...], wv_ref[...])
    ).astype(BF16)
    split_halves(me_ref, part_ref, keep_ref, send_ref)


def finish_kernel(
    me_ref,
    scal_ref,
    normed_own_ref,
    normed_other_ref,
    mlp_own_ref,
    mlp_other_ref,
    second_own_ref,
    second_other_ref,
    layer_ref,
    hid_ref,
    ghid_ref,
    norm_ref,
    out_ref,
    gin_ref,
    sums_ref,
):
    half = mlp_own_ref.shape[0]
    bit = me_ref[1] & 1
    weight = scal_ref[0]
    step = 32
    sums_ref[...] = jnp.zeros_like(sums_ref)
    for first_ref, mlp_ref, second_ref, which in (
        (normed_other_ref, mlp_other_ref, second_other_ref, 1 - bit),
        (normed_own_ref, mlp_own_ref, second_own_ref, bit),
    ):
        start = pl.multiple_of(which * half, half)

        @pl.loop(0, half // step)
        def _(i, first_ref=first_ref, mlp_ref=mlp_ref, second_ref=second_ref, start=start):
            at = pl.multiple_of(i * step, step)
            here = pl.ds(at, step)
            rows = pl.ds(pl.multiple_of(start + at, step), step)
            hid = hid_ref[rows, :]
            out_ref[rows, :] = hid + mlp_ref[here, :].astype(F32)
            hat, inv_std = norm_hat(layer_ref[rows, :])
            grad = first_ref[here, :].astype(F32)
            gin_ref[rows, :] = ghid_ref[rows, :] + norm_back(grad, hat, inv_std, norm_ref[0:1, :])
            hat2, _ = norm_hat(hid)
            grad2 = second_ref[here, :].astype(F32)
            sums_ref[0:8, :] += jnp.sum((grad * hat).reshape(step // 8, 8, D), axis=0)
            sums_ref[8:16, :] += jnp.sum(grad.reshape(step // 8, 8, D), axis=0)
            sums_ref[16:24, :] += jnp.sum((grad2 * hat2).reshape(step // 8, 8, D), axis=0)
            sums_ref[24:32, :] += jnp.sum(grad2.reshape(step // 8, 8, D), axis=0)

    total = [
        jnp.sum(sums_ref[8 * i : 8 * i + 8, :], axis=0, keepdims=True) * weight for i in range(4)
    ]
    total.append(jnp.full((1, D), weight, F32))
    total.append(jnp.zeros((3, D), F32))
    sums_ref[0:8, :] = jnp.concatenate(total, axis=0)


def reflect(matrix, left, right):
    coef_left = 2.0 / jnp.sum(left[:, 0:1] * left[:, 0:1])
    coef_right = 2.0 / jnp.sum(right * right)
    matrix = matrix - (coef_left * left) * jnp.sum(left * matrix, axis=0, keepdims=True)
    return matrix - (coef_right * right) * jnp.sum(matrix * right, axis=1, keepdims=True)


def column(row):
    return jnp.transpose(jnp.broadcast_to(row, (BLK, BLK)))


def rotate_kernel(chunks, norm_ref, left_ref, right_ref, *rest):
    parts = rest[: 2 * len(chunks)]
    grad_ref, rot_ref, square_ref = rest[2 * len(chunks) :]
    inverse = 1.0 / norm_ref[4:5, 0:BLK]
    slot = 0
    square = jnp.zeros((8, BLK), F32)
    for number, count in enumerate(chunks):
        keep_ref, recv_ref = parts[2 * number : 2 * number + 2]
        for j in range(count):
            grad = (keep_ref[j].astype(F32) + recv_ref[j].astype(F32)) * inverse
            grad_ref[slot] = grad
            square = square + jnp.sum((grad * grad).reshape(BLK // 8, 8, BLK), axis=0)
            rot_ref[slot] = reflect(
                grad, column(left_ref[slot : slot + 1, :]), right_ref[slot : slot + 1, :]
            )
            slot += 1
    square_ref[...] = jnp.full((8, BLK), jnp.sum(square), F32)


def update_kernel(
    group,
    scal_ref,
    square_ref,
    sums_ref,
    norm_ref,
    norm_first_ref,
    norm_second_ref,
    left_ref,
    right_ref,
    grad_ref,
    rot_ref,
    first_ref,
    second_ref,
    master_ref,
    out_grad_ref,
    out_first_ref,
    out_second_ref,
    out_master_ref,
    out_copy_ref,
    norm_pair_ref,
    norm_square_ref,
    norm_value_ref,
    clip_ref,
):
    inv_one = 1.0 / scal_ref[1]
    inv_two = 1.0 / scal_ref[2]
    norm_grad = sums_ref[0:4, :] * (1.0 / sums_ref[4:5, :])
    total = square_ref[0:1, :] + jnp.sum(norm_grad * norm_grad)
    clip_norm = jnp.sqrt(total)
    factor = jnp.minimum(1.0, clip_max / clip_norm)
    at = pl.program_id(0)

    @pl.when(at == 0)
    def _():
        clip_ref[...] = jnp.broadcast_to(clip_norm, clip_ref.shape)
        clipped = norm_grad * factor[:, 0:1]
        first = beta_one * norm_first_ref[...] + (1.0 - beta_one) * clipped
        second = beta_two * norm_second_ref[...] + (1.0 - beta_two) * clipped * clipped
        norm_pair_ref[0] = clipped
        norm_pair_ref[1] = first
        norm_square_ref[...] = second
        norm_value_ref[...] = norm_ref[...] - step_rate * (first * inv_one) / (
            jnp.sqrt(second * inv_two) + adam_eps
        )

    for i in range(group):
        slot = at * group + i
        left = column(left_ref[pl.ds(slot, 1), :])
        right = right_ref[pl.ds(slot, 1), :]
        out_grad_ref[i] = grad_ref[i] * factor
        rotated = rot_ref[i] * factor
        first = beta_one * first_ref[i] + (1.0 - beta_one) * rotated
        second = beta_two * second_ref[i] + (1.0 - beta_two) * rotated * rotated
        out_first_ref[i] = first
        out_second_ref[i] = second
        normal = (first * inv_one) / (jnp.sqrt(second * inv_two) + adam_eps)
        turned = reflect(normal, left, right)
        master = master_ref[i]
        entries = 1.0 / (BLK * BLK)
        trust = jnp.sqrt(jnp.sum(master * master) * entries + trust_eps) / jnp.sqrt(
            jnp.sum(turned * turned) * entries + trust_eps
        )
        fresh = master - (step_rate * trust) * turned
        out_master_ref[i] = fresh
        out_copy_ref[i] = fresh.astype(BF16)


def vmem():
    return pl.BlockSpec(memory_space=pltpu.VMEM)


def smem():
    return pl.BlockSpec(memory_space=pltpu.SMEM)


def call(kernel, name, n_smem, ins, outs, scratch=(), flops=0):
    return pl.pallas_call(
        kernel,
        name=name,
        out_shape=[jax.ShapeDtypeStruct(shape, kind) for shape, kind in outs],
        in_specs=[smem()] * n_smem + [vmem()] * (len(ins) - n_smem),
        out_specs=[vmem()] * len(outs),
        scratch_shapes=[pltpu.VMEM(shape, kind) for shape, kind in scratch],
        compiler_params=pltpu.CompilerParams(vmem_limit_bytes=VMEM_LIMIT),
        cost_estimate=pl.CostEstimate(flops=int(flops), bytes_accessed=4 << 20, transcendentals=0),
    )(*ins)


def swap(value, axis, bit):
    count = lax.axis_size(axis)
    return lax.ppermute(value, axis, [(i, i ^ bit) for i in range(count)])


def plus(left, right):
    return (left.astype(F32) + right.astype(F32)).astype(BF16)


def mp_sum(keep, send):
    total = plus(keep, swap(send, "mp", 1))
    bit = 2
    while bit < lax.axis_size("mp"):
        total = plus(total, swap(total, "mp", bit))
        bit *= 2
    return (total, swap(total, "mp", 1))


def split_counts(slots):
    if slots >= 12:
        tail = slots // 6
        head = (slots - tail) // 2
        return (slots - tail - head, head, tail)
    return (1,) * slots if slots <= 3 else (slots - slots // 2, slots // 2)


def shards(
    tokens,
    cotangent,
    segment_ids,
    table_index,
    group_count,
    owner_list,
    step_count,
    query_weight,
    key_weight,
    value_weight,
    output_weight,
    hidden_weight,
    return_weight,
    norm_params,
    norm_first,
    norm_second,
    master_blocks,
    first_moment,
    second_moment,
    left_vector,
    right_vector,
):
    length = tokens.shape[0]
    half = length // 2
    width = query_weight.shape[1]
    units = hidden_weight.shape[1]
    slots = master_blocks.shape[0]
    blocks = owner_list.shape[0]
    n_dp = lax.axis_size("dp")
    me = jnp.stack([lax.axis_index("dp"), lax.axis_index("mp")]).astype(jnp.int32)
    step_value = step_count[0].astype(F32)
    scal = jnp.stack(
        [
            group_count[0].astype(F32),
            1.0 - jnp.power(beta_one, step_value),
            1.0 - jnp.power(beta_two, step_value),
        ]
    )
    seg_row = segment_ids.reshape(1, length)
    index_row = table_index.reshape(1, length)
    table = jnp.asarray(position_rows())
    rows_d = (length, D)
    half_d = (half, D)
    unit = 2 * length * D * D

    layer_in, normed, q, k, v, mixed, lse, bias, keep, send = call(
        forward_kernel,
        "attention_forward",
        1,
        (
            me,
            tokens,
            index_row,
            seg_row,
            table,
            norm_params,
            query_weight,
            key_weight,
            value_weight,
            output_weight,
        ),
        [
            (rows_d, F32),
            (rows_d, BF16),
            ((length, width), BF16),
            ((length, width), BF16),
            ((length, width), BF16),
            ((length, width), BF16),
            ((length, width // HEAD), F32),
            ((length, length), F32),
            (half_d, BF16),
            (half_d, BF16),
        ],
        [(rows_d, BF16)],
        flops=5 * unit,
    )
    attn_own, attn_other = mp_sum(keep, send)
    grad_out, grad_act = call(
        grad_out_kernel,
        "grad_of_act",
        0,
        (cotangent, seg_row, return_weight),
        [(rows_d, BF16), ((length, units), F32)],
        flops=2 * unit,
    )
    hidden_in, second, act, grad_pre, keep, send = call(
        feed_kernel,
        "feed_forward",
        1,
        (me, attn_own, attn_other, layer_in, norm_params, hidden_weight, grad_act),
        [
            (rows_d, F32),
            (rows_d, BF16),
            ((length, units), BF16),
            ((length, units), BF16),
            (half_d, BF16),
            (half_d, BF16),
        ],
        [((half, units), F32)],
        flops=8 * unit,
    )
    second_own, second_other = mp_sum(keep, send)
    nat, keep, send = call(
        feed_grad_kernel,
        "feed_weight_grads",
        2,
        (me, scal, act, grad_out, second, grad_pre, return_weight),
        [((blocks - blocks // 3, BLK, BLK), BF16), (half_d, BF16), (half_d, BF16)],
        [(rows_d, BF16)],
        flops=6 * unit,
    )
    mlp_own, mlp_other = mp_sum(keep, send)
    chunks = split_counts(slots)
    chunk_shapes = []
    for count in chunks:
        chunk_shapes += [((n_dp // 2 * count, BLK, BLK), BF16)] * 2
    ins = (
        me,
        owner_list,
        scal,
        second_own,
        second_other,
        hidden_in,
        grad_out,
        norm_params,
        normed,
        q,
        k,
        v,
        mixed,
        lse,
        bias,
        output_weight,
        nat,
    )
    outs = call(
        functools.partial(backward_kernel, chunks, n_dp),
        "attention_backward",
        3,
        ins,
        [
            (rows_d, F32),
            ((length, width), BF16),
            ((length, width), BF16),
            ((length, width), BF16),
        ]
        + chunk_shapes,
        [(rows_d, BF16), ((length, width), BF16), ((blocks // 3, BLK, BLK), BF16)],
        flops=10 * unit,
    )
    grad_hid, gq, gk, gv = outs[:4]
    chunk_arrays = outs[4:]
    keep, send = call(
        normed_grad_kernel,
        "grad_of_normed",
        1,
        (me, gq, gk, gv, query_weight, key_weight, value_weight),
        [(half_d, BF16), (half_d, BF16)],
        [(rows_d, BF16)],
        flops=unit,
    )
    normed_own, normed_other = mp_sum(keep, send)

    state = [(chunk_arrays[2 * i], chunk_arrays[2 * i + 1]) for i in range(len(chunks))]
    pending = []
    for keep, send in state:
        bit = 1
        while True:
            got = swap(send, "dp", bit)
            bit *= 2
            if bit >= n_dp:
                break
            n = keep.shape[0] // 2
            keep, send = plus(keep[:n], got[:n]), plus(keep[n:], got[n:])
        pending += [keep, got]

    out, input_grad, sums = call(
        finish_kernel,
        "layer_outputs",
        2,
        (
            me,
            scal,
            normed_own,
            normed_other,
            mlp_own,
            mlp_other,
            second_own,
            second_other,
            layer_in,
            hidden_in,
            grad_hid,
            norm_params,
        ),
        [(rows_d, F32), (rows_d, F32), ((32, D), F32)],
        flops=2 * unit,
    )
    sums = sums[0:8]
    bit = 1
    while bit < n_dp:
        sums = sums + swap(sums, "dp", bit)
        bit *= 2
    left = left_vector.reshape(slots, BLK)
    right = right_vector.reshape(slots, BLK)
    grads, rotated, square = call(
        functools.partial(rotate_kernel, chunks),
        "rotate",
        0,
        (sums, left, right, *pending),
        [((slots, BLK, BLK), F32), ((slots, BLK, BLK), F32), ((8, BLK), F32)],
        flops=unit,
    )
    for axis in ("mp", "dp"):
        bit = 1
        while bit < lax.axis_size(axis):
            square = square + swap(square, axis, bit)
            bit *= 2
    group = max(g for g in range(1, 7) if slots % g == 0)
    block_spec = pl.BlockSpec((group, BLK, BLK), lambda i: (i, 0, 0))

    def whole(shape):
        return pl.BlockSpec(shape, lambda i: (0,) * len(shape))

    shape_block = jax.ShapeDtypeStruct((slots, BLK, BLK), F32)
    new = pl.pallas_call(
        functools.partial(update_kernel, group),
        name="update",
        grid=(slots // group,),
        out_shape=[shape_block] * 4
        + [
            jax.ShapeDtypeStruct((slots, BLK, BLK), BF16),
            jax.ShapeDtypeStruct((2, 4, D), F32),
            jax.ShapeDtypeStruct((4, D), F32),
            jax.ShapeDtypeStruct((4, D), F32),
            jax.ShapeDtypeStruct((8, BLK), F32),
        ],
        in_specs=[
            smem(),
            whole((8, BLK)),
            whole((8, D)),
            whole((4, D)),
            whole((4, D)),
            whole((4, D)),
            whole((slots, BLK)),
            whole((slots, BLK)),
        ]
        + [block_spec] * 5,
        out_specs=[block_spec] * 5
        + [whole((2, 4, D)), whole((4, D)), whole((4, D)), whole((8, BLK))],
        compiler_params=pltpu.CompilerParams(vmem_limit_bytes=VMEM_LIMIT),
    )(
        scal,
        square,
        sums,
        norm_params,
        norm_first,
        norm_second,
        left,
        right,
        grads,
        rotated,
        first_moment.reshape(slots, BLK, BLK),
        second_moment.reshape(slots, BLK, BLK),
        master_blocks.reshape(slots, BLK, BLK),
    )
    shard_shape = (slots, 1, BLK, BLK)
    return (
        out,
        input_grad,
        new[0].reshape(shard_shape),
        new[1].reshape(shard_shape),
        new[2].reshape(shard_shape),
        new[3].reshape(shard_shape),
        new[4].reshape(shard_shape),
        new[5],
        new[6],
        new[7],
        new[8][0, 0],
    )


def solution(mesh):
    placed = (
        P("dp", None),
        P("dp", None),
        P("dp"),
        P("dp"),
        P("dp"),
        P(),
        P(),
        P(None, "mp"),
        P(None, "mp"),
        P(None, "mp"),
        P("mp", None),
        P(None, "mp"),
        P("mp", None),
        P(),
        P(),
        P(),
        P("dp", "mp", None, None),
        P("dp", "mp", None, None),
        P("dp", "mp", None, None),
        P("dp", "mp", None),
        P("dp", "mp", None),
    )
    return jax.shard_map(
        shards,
        mesh=mesh,
        in_specs=placed,
        out_specs=(
            P("dp", None),
            P("dp", None),
            P("dp", "mp", None, None),
            P("dp", "mp", None, None),
            P("dp", "mp", None, None),
            P("dp", "mp", None, None),
            P("dp", "mp", None, None),
            P(),
            P(),
            P(),
            P(),
        ),
        check_vma=False,
    )
```

time: 681 us -> 250 us (0.37); the launches traced: 673 us -> 249 us
  waiting for transfers between devices: 411 us -> 130 us
  blocking collectives: 80.5 us -> 0 us
  Pallas kernels: 0 us -> 75.8 us
  other arithmetic: 64.5 us -> 3.51 us
  matrix products: 50.2 us -> 0 us
  local copies, waits for them, and re-layouts: 47.1 us -> 9.1 us
  starting transfers between devices: 0.8 us -> 28.6 us
  between operations: 19.5 us -> 2.38 us
    psum x4 -> x0, waiting for transfers between devices: 411 us -> none  [the longest x1 353 us: shards(): summed = lax.psum(ordered, 'dp')]
    ppermute x0 -> x29, waiting for transfers between devices: none -> 130 us  [swap(): return lax.ppermute(value, axis, [(i, i ^ bit) for i in range(count)])]
    psum x2 -> x0, blocking collectives: 80.5 us -> none  [the longest x1 41.2 us: shards(): norm_total, count_total = lax.psum((norm_grads * weight, weight), 'dp')]
    pallas_call x0 -> x9, Pallas kernels: none -> 75.8 us  [the longest x8 62.3 us: call(): pl.pallas_call(kernel, name=name, out_shape=[jax.ShapeDtypeStruct(shape,...]
    dot_general x28 -> x0, matrix products: 50.2 us -> none  [the longest x6 10.5 us: inner_rows(): lax.dot_general(left, right, (((0,), (0,)), ((), ())), preferred_element_...]
    ppermute x0 -> x29, starting transfers between devices: none -> 28.6 us  [swap(): return lax.ppermute(value, axis, [(i, i ^ bit) for i in range(count)])]
    reduce_sum x13 -> x0, other arithmetic: 15.8 us -> none  [the longest x1 3.09 us: shards(): jnp.sum(owned * owned)]
    gather x1 -> x0, local copies, waits for them, and re-layouts: 15.4 us -> none  [shards(): ordered = jnp.take(local_blocks, owner_list, axis=0)]
  transfers between devices with their start and end apart: 4 -> 29, of which waited for: 3 -> 16; matrix products, arithmetic and copies ran while one was open for 11% -> 1% of each run, Pallas kernels for 0% -> 15%
where the time goes in v1:
time: 250 us; the launch traced here: 249 us
  waiting for transfers between devices  130 us (52%)
  Pallas kernels  75.8 us (30%)
  starting transfers between devices  28.6 us (11%)
  local copies, waits for them, and re-layouts  9.1 us (4%)
  other arithmetic  3.51 us (1%)
    ppermute x29, waiting for transfers between devices, swap(): return lax.ppermute(value, axis, [(i, i ^ bit) for i in range(count)])  130 us
    pallas_call x8, Pallas kernels, call(): pl.pallas_call(kernel, name=name, out_shape=[jax.ShapeDtypeStruct(shape,...  62.3 us
    ppermute x29, starting transfers between devices, swap(): return lax.ppermute(value, axis, [(i, i ^ bit) for i in range(count)])  28.6 us
    pallas_call x1, Pallas kernels, shards(): pl.pallas_call(functools.partial(update_kernel, group), name='update', gr...  13.5 us
    unnamed x56, local copies, waits for them, and re-layouts  8.59 us
  transfers between devices with their start and end apart: 29, of which 16 were waited for; matrix products, arithmetic and copies ran while one was open for 1% of the time, Pallas kernels for 15%

profile of v1, /device:TPU:0, one launch (start us, length us, event | category | flops | bytes accessed | tf_op | source)
XLA Modules:
  0.0 249.5 jit_solution(425936984284239854)
XLA Ops:
  7.9 9.5 %attention_forward.1 = (f32[512,1024]{1,0:T(8,128)}, bf16[512,1024]{1,0:T(8,128)(2,1)S(1)}, bf16[512,256]{1,0:T(8,128)(2,1)S(1)}, bf16[512,256]{1,0:T(8,128)(2,1...) custom-call(s32[2]{0:T(128)S(1)} %pad_add_fusion.me_ref, ...), custom_call_target="tpu_custom_call" | custom-call | flops 5368709120 | bytes 4194304 | tf_op jit(solution)/shard_map/attention_forward/pallas_call | solution.py:562
  19.6 2.9 %collective-permute-start.1 = (bf16[256,1024]{1,0:T(8,128)(2,1)S(1)}, bf16[256,1024]{1,0:T(8,128)(2,1)S(1)}, u32[]{:S(2)}, u32[]{:S(2)}) collective-permute-start(bf16[256,1024]{1,0:T(8,128)(2,1)S(1)} %add_convert_fusion.11), channel_id=1, source_target_pairs={{0,2},{1,3},{2,0},{3,1},{4,6},{5,7},{6,4},{7,5},{8,10},{9,11},{10,... | collective-permute-start | bytes 1572872 | tf_op jit(solution)/shard_map/ppermute | solution.py:576
  22.5 12.2 %collective-permute-done.1 = bf16[256,1024]{1,0:T(8,128)(2,1)S(1)} collective-permute-done((bf16[256,1024]{1,0:T(8,128)(2,1)S(1)}, bf16[256,1024]{1,0:T(8,128)(2,1)S(1)}, u32[]{:S(2)}, u32[]{:S(2)}) %collective-permute-start.1) | collective-permute-done | bytes 524320 | tf_op jit(solution)/shard_map/ppermute | solution.py:576
  35.1 3.0 %grad_of_act.1 = (bf16[512,1024]{1,0:T(8,128)(2,1)S(1)}, f32[512,1024]{1,0:T(8,128)S(1)}) custom-call(bf16[512,1024]{1,0:T(8,128)(2,1)S(1)} %copy-done.8, s32[1,512]{1,0:T(1,128)S(1)} %bitcast.32, bf16[1024,1024]{1,0:T(8,128)(2,1)} %wr_ref.3), custom_call_target="tpu_custom_call" | custom-call | flops 2147483648 | bytes 4194304 | tf_op jit(solution)/shard_map/grad_of_act/pallas_call | solution.py:562
  39.4 10.7 %feed_forward.1 = (f32[512,1024]{1,0:T(8,128)}, bf16[512,1024]{1,0:T(8,128)(2,1)S(1)}, bf16[512,1024]{1,0:T(8,128)(2,1)S(1)}, bf16[512,1024]{1,0:T(8,128)(2,1)S(...) custom-call(s32[2]{0:T(128)S(1)} %pad_add_fusion.me_ref, ...), custom_call_target="tpu_custom_call" | custom-call | flops 8589934592 | bytes 4194304 | tf_op jit(solution)/shard_map/feed_forward/pallas_call | solution.py:562
  55.6 11.0 %collective-permute-done.4 = bf16[256,1024]{1,0:T(8,128)(2,1)S(1)} collective-permute-done((bf16[256,1024]{1,0:T(8,128)(2,1)S(1)}, bf16[256,1024]{1,0:T(8,128)(2,1)S(1)}, u32[]{:S(2)}, u32[]{:S(2)}) %collective-permute-start.4) | collective-permute-done | bytes 524320 | tf_op jit(solution)/shard_map/ppermute | solution.py:576
  66.9 6.5 %feed_weight_grads.1 = (bf16[128,128,128]{2,1,0:T(8,128)(2,1)}, bf16[256,1024]{1,0:T(8,128)(2,1)S(1)}, bf16[256,1024]{1,0:T(8,128)(2,1)S(1)}) custom-call(s32[2]{0:T(128)S(1)} %pad_add_fusion.me_ref, f32[3]{0:T(128)S(1)} %pad_maximum_fusion.scal_ref, bf16[512,1024]{1,0:T(8,128)(2,1)S(1)} %get-tuple-element.74.act_ref, ...), custom_call_target="tpu_custom_call" | custom-call | flops 6442450944 | bytes 4194304 | tf_op jit(solution)/shard_map/feed_weight_grads/pallas_call | solution.py:562
  73.9 18.2 %attention_backward.1 = (f32[512,1024]{1,0:T(8,128)}, bf16[512,256]{1,0:T(8,128)(2,1)S(1)}, bf16[512,256]{1,0:T(8,128)(2,1)S(1)}, bf16[512,256]{1,0:T(8,128)(2,1...) custom-call(s32[2]{0:T(128)S(1)} %pad_add_fusion.me_ref, ...), custom_call_target="tpu_custom_call" | custom-call | flops 10737418240 | bytes 4194304 | tf_op jit(solution)/shard_map/attention_backward/pallas_call | solution.py:562
  98.7 12.1 %collective-permute-done.10 = bf16[256,1024]{1,0:T(8,128)(2,1)S(1)} collective-permute-done((bf16[256,1024]{1,0:T(8,128)(2,1)S(1)}, bf16[256,1024]{1,0:T(8,128)(2,1)S(1)}, u32[]{:S(2)}, u32[]{:S(2)}) %collective-permute-start.10) | collective-permute-done | bytes 524320 | tf_op jit(solution)/shard_map/ppermute | solution.py:576
  111.4 9.8 %collective-permute-done.7 = bf16[256,1024]{1,0:T(8,128)(2,1)S(1)} collective-permute-done((bf16[256,1024]{1,0:T(8,128)(2,1)S(1)}, bf16[256,1024]{1,0:T(8,128)(2,1)S(1)}, u32[]{:S(2)}, u32[]{:S(2)}) %collective-permute-start.7) | collective-permute-done | bytes 524320 | tf_op jit(solution)/shard_map/ppermute | solution.py:576
  121.5 4.0 %collective-permute-done.15 = bf16[40,128,128]{2,1,0:T(8,128)(2,1)S(1)} collective-permute-done((bf16[40,128,128]{2,1,0:T(8,128)(2,1)S(1)}, bf16[40,128,128]{2,1,0:T(8,128)(2,1)S(1)}, u32[]{:S(2)}, u32[]{:S(2)}) %collective-permute-start.15) | collective-permute-done | bytes 1310752 | tf_op jit(solution)/shard_map/ppermute | solution.py:576
  127.9 25.7 %collective-permute-done.18 = bf16[40,128,128]{2,1,0:T(8,128)(2,1)S(1)} collective-permute-done((bf16[40,128,128]{2,1,0:T(8,128)(2,1)S(1)}, bf16[40,128,128]{2,1,0:T(8,128)(2,1)S(1)}, u32[]{:S(2)}, u32[]{:S(2)}) %collective-permute-start.18) | collective-permute-done | bytes 1310752 | tf_op jit(solution)/shard_map/ppermute | solution.py:576
  156.0 8.4 %collective-permute-done.21 = bf16[16,128,128]{2,1,0:T(8,128)(2,1)S(1)} collective-permute-done((bf16[16,128,128]{2,1,0:T(8,128)(2,1)S(1)}, bf16[16,128,128]{2,1,0:T(8,128)(2,1)S(1)}, u32[]{:S(2)}, u32[]{:S(2)}) %collective-permute-start.21) | collective-permute-done | bytes 524320 | tf_op jit(solution)/shard_map/ppermute | solution.py:576
  166.7 9.0 %layer_outputs.1 = (f32[512,1024]{1,0:T(8,128)}, f32[512,1024]{1,0:T(8,128)}, f32[32,1024]{1,0:T(8,128)S(1)}) custom-call(s32[2]{0:T(128)S(1)} %pad_add_fusion.me_ref, f32[3]{0:T(128)S(1)} %pad_maximum_fusion.scal_ref, bf16[256,1024]{1,0:T(8,128)(2,1)S(1)} %add_convert_fusion.6.normed_own_ref, bf16[256,1024]{1,0:T(8,128)(2,1)S(1)} %collective-permute-done.8.normed_other_ref, ...), custom_call_target="tpu_custom_call" | custom-call | flops 2147483648 | bytes 4194304 | tf_op jit(solution)/shard_map/layer_outputs/pallas_call | solution.py:562
  177.5 2.7 %collective-permute-start.17 = (bf16[10,128,128]{2,1,0:T(8,128)(2,1)S(1)}, bf16[10,128,128]{2,1,0:T(8,128)(2,1)S(1)}, u32[]{:S(2)}, u32[]{:S(2)}) collective-permute-start(bf16[10,128,128]{2,1,0:T(8,128)(2,1)S(1)} %get-tuple-element.124), channel_id=1, source_target_pairs={{0,16},{4,20},{8,24},{12,28},{16,0},{20,4},{24,8},{28,12},{1,17},{... | collective-permute-start | bytes 983048 | tf_op jit(solution)/shard_map/ppermute | solution.py:576
  180.8 2.7 %collective-permute-start.23 = (bf16[4,128,128]{2,1,0:T(8,128)(2,1)S(1)}, bf16[4,128,128]{2,1,0:T(8,128)(2,1)S(1)}, u32[]{:S(2)}, u32[]{:S(2)}) collective-permute-start(bf16[4,128,128]{2,1,0:T(8,128)(2,1)S(1)} %get-tuple-element.128), channel_id=1, source_target_pairs={{0,16},{4,20},{8,24},{12,28},{16,0},{20,4},{24,8},{28,12},{1,17},{... | collective-permute-start | bytes 393224 | tf_op jit(solution)/shard_map/ppermute | solution.py:576
  184.0 13.3 %collective-permute-done.13 = f32[8,1024]{1,0:T(8,128)S(1)} collective-permute-done((f32[8,1024]{1,0:T(8,128)S(1)}, f32[8,1024]{1,0:T(8,128)S(1)}, u32[]{:S(2)}, u32[]{:S(2)}) %collective-permute-start.13) | collective-permute-done | bytes 32800 | tf_op jit(solution)/shard_map/ppermute | solution.py:576
  198.2 16.9 %collective-permute-done.14 = f32[8,1024]{1,0:T(8,128)S(1)} collective-permute-done((f32[8,1024]{1,0:T(8,128)S(1)}, f32[8,1024]{1,0:T(8,128)S(1)}, u32[]{:S(2)}, u32[]{:S(2)}) %collective-permute-start.14) | collective-permute-done | bytes 32800 | tf_op jit(solution)/shard_map/ppermute | solution.py:576
  215.2 3.7 %rotate.1 = (f32[24,128,128]{2,1,0:T(8,128)S(1)}, f32[24,128,128]{2,1,0:T(8,128)S(1)}, f32[8,128]{1,0:T(8,128)S(1)}) custom-call(f32[8,1024]{1,0:T(8,128)S(1)} %add.94.norm_ref.sums_ref, f32[24,128]{1,0:T(8,128)S(1)} %bitcast.26, f32[24,128]{1,0:T(8,128)S(1)} %bitcast.28, bf16[10,128,128]{2,1,0:T(8,128)(2,1)S(1)} %get-tuple-element.125.rest_0_, ...), custom_call_target="tpu_custom_call" | custom-call | flops 1073741824 | bytes 4194304 | tf_op jit(solution)/shard_map/rotate/pallas_call | solution.py:562
  221.7 2.1 collective-permute-done.25
  224.2 3.1 %collective-permute-done.26 = f32[8,128]{1,0:T(8,128)S(1)} collective-permute-done((f32[8,128]{1,0:T(8,128)S(1)}, f32[8,128]{1,0:T(8,128)S(1)}, u32[]{:S(2)}, u32[]{:S(2)}) %collective-permute-start.26) | collective-permute-done | bytes 4128 | tf_op jit(solution)/shard_map/ppermute | solution.py:576
  227.4 3.6 %collective-permute-done.27 = f32[8,128]{1,0:T(8,128)S(1)} collective-permute-done((f32[8,128]{1,0:T(8,128)S(1)}, f32[8,128]{1,0:T(8,128)S(1)}, u32[]{:S(2)}, u32[]{:S(2)}) %collective-permute-start.27) | collective-permute-done | bytes 4128 | tf_op jit(solution)/shard_map/ppermute | solution.py:576
  232.1 3.4 %collective-permute-done.28 = f32[8,128]{1,0:T(8,128)S(1)} collective-permute-done((f32[8,128]{1,0:T(8,128)S(1)}, f32[8,128]{1,0:T(8,128)S(1)}, u32[]{:S(2)}, u32[]{:S(2)}) %collective-permute-start.28) | collective-permute-done | bytes 4128 | tf_op jit(solution)/shard_map/ppermute | solution.py:576
  235.5 13.5 %update.1 = (f32[24,128,128]{2,1,0:T(8,128)}, f32[24,128,128]{2,1,0:T(8,128)}, f32[24,128,128]{2,1,0:T(8,128)}, f32[24,128,128]{2,1,0:T(8,128)}, bf16[24,128,128...) custom-call(f32[3]{0:T(128)S(1)} %pad_maximum_fusion.scal_ref, ...), custom_call_target="tpu_custom_call" | custom-call | tf_op jit(solution)/shard_map/update/pallas_call | solution.py:825
  (125 shorter events, 38.9 us)
Async XLA Ops:
  19.6 15.2 %collective-permute-start.1 = (bf16[256,1024]{1,0:T(8,128)(2,1)S(1)}, bf16[256,1024]{1,0:T(8,128)(2,1)S(1)}, u32[]{:S(2)}, u32[]{:S(2)}) collective-permute-start(bf16[256,1024]{1,0:T(8,128)(2,1)S(1)} %add_convert_fusion.11), channel_id=1, source_target_pairs={{0,2},{1,3},{2,0},{3,1},{4,6},{5,7},{6,4},{7,5},{8,10},{9,11},{10,... | collective-permute-start | bytes 1572872 | tf_op jit(solution)/shard_map/ppermute | solution.py:576
  35.0 4.5 %collective-permute-start.2 = (bf16[256,1024]{1,0:T(8,128)(2,1)S(1)}, bf16[256,1024]{1,0:T(8,128)(2,1)S(1)}, u32[]{:S(2)}, u32[]{:S(2)}) collective-permute-start(bf16[256,1024]{1,0:T(8,128)(2,1)S(1)} %add_convert_fusion.10.own_ref), channel_id=1, source_target_pairs={{0,1},{1,0},{2,3},{3,2},{4,5},{5,4},{6,7},{7,6},{8,9},{9,8},{10,11... | collective-permute-start | bytes 1572872 | tf_op jit(solution)/shard_map/ppermute | solution.py:576
  52.4 14.3 %collective-permute-start.4 = (bf16[256,1024]{1,0:T(8,128)(2,1)S(1)}, bf16[256,1024]{1,0:T(8,128)(2,1)S(1)}, u32[]{:S(2)}, u32[]{:S(2)}) collective-permute-start(bf16[256,1024]{1,0:T(8,128)(2,1)S(1)} %add_convert_fusion.9), channel_id=1, source_target_pairs={{0,2},{1,3},{2,0},{3,1},{4,6},{5,7},{6,4},{7,5},{8,10},{9,11},{10,... | collective-permute-start | bytes 1572872 | tf_op jit(solution)/shard_map/ppermute | solution.py:576
  66.8 7.0 %collective-permute-start.5 = (bf16[256,1024]{1,0:T(8,128)(2,1)S(1)}, bf16[256,1024]{1,0:T(8,128)(2,1)S(1)}, u32[]{:S(2)}, u32[]{:S(2)}) collective-permute-start(bf16[256,1024]{1,0:T(8,128)(2,1)S(1)} %add_convert_fusion.8.own_ref.second_own_ref), channel_id=1, source_target_pairs={{0,1},{1,0},{2,3},{3,2},{4,5},{5,4},{6,7},{7,6},{8,9},{9,8},{10,11... | collective-permute-start | bytes 1572872 | tf_op jit(solution)/shard_map/ppermute | solution.py:576
  73.4 22.3 %collective-permute-start.9 = (bf16[256,1024]{1,0:T(8,128)(2,1)S(1)}, bf16[256,1024]{1,0:T(8,128)(2,1)S(1)}, u32[]{:S(2)}, u32[]{:S(2)}) collective-permute-start(bf16[256,1024]{1,0:T(8,128)(2,1)S(1)} %get-tuple-element.84), channel_id=1, source_target_pairs={{0,1},{1,0},{2,3},{3,2},{4,5},{5,4},{6,7},{7,6},{8,9},{9,8},{10,11... | collective-permute-start | bytes 1572872 | tf_op jit(solution)/shard_map/ppermute | solution.py:576
  93.8 4.2 %collective-permute-start.6 = (bf16[256,1024]{1,0:T(8,128)(2,1)S(1)}, bf16[256,1024]{1,0:T(8,128)(2,1)S(1)}, u32[]{:S(2)}, u32[]{:S(2)}) collective-permute-start(bf16[256,1024]{1,0:T(8,128)(2,1)S(1)} %get-tuple-element.82), channel_id=1, source_target_pairs={{0,1},{1,0},{2,3},{3,2},{4,5},{5,4},{6,7},{7,6},{8,9},{9,8},{10,11... | collective-permute-start | bytes 1572872 | tf_op jit(solution)/shard_map/ppermute | solution.py:576
  93.9 31.6 %collective-permute-start.15 = (bf16[40,128,128]{2,1,0:T(8,128)(2,1)S(1)}, bf16[40,128,128]{2,1,0:T(8,128)(2,1)S(1)}, u32[]{:S(2)}, u32[]{:S(2)}) collective-permute-start(bf16[40,128,128]{2,1,0:T(8,128)(2,1)S(1)} %copy-done.27), channel_id=1, source_target_pairs={{0,4},{4,0},{8,12},{12,8},{16,20},{20,16},{24,28},{28,24},{1,5},{5... | collective-permute-start | bytes 3932168 | tf_op jit(solution)/shard_map/ppermute | solution.py:576
  96.0 14.8 %collective-permute-start.10 = (bf16[256,1024]{1,0:T(8,128)(2,1)S(1)}, bf16[256,1024]{1,0:T(8,128)(2,1)S(1)}, u32[]{:S(2)}, u32[]{:S(2)}) collective-permute-start(bf16[256,1024]{1,0:T(8,128)(2,1)S(1)} %add_convert_fusion.5), channel_id=1, source_target_pairs={{0,2},{1,3},{2,0},{3,1},{4,6},{5,7},{6,4},{7,5},{8,10},{9,11},{10,... | collective-permute-start | bytes 1572872 | tf_op jit(solution)/shard_map/ppermute | solution.py:576
  97.5 56.1 %collective-permute-start.18 = (bf16[40,128,128]{2,1,0:T(8,128)(2,1)S(1)}, bf16[40,128,128]{2,1,0:T(8,128)(2,1)S(1)}, u32[]{:S(2)}, u32[]{:S(2)}) collective-permute-start(bf16[40,128,128]{2,1,0:T(8,128)(2,1)S(1)} %copy-done.26), channel_id=1, source_target_pairs={{0,4},{4,0},{8,12},{12,8},{16,20},{20,16},{24,28},{28,24},{1,5},{5... | collective-permute-start | bytes 3932168 | tf_op jit(solution)/shard_map/ppermute | solution.py:576
  98.2 23.0 %collective-permute-start.7 = (bf16[256,1024]{1,0:T(8,128)(2,1)S(1)}, bf16[256,1024]{1,0:T(8,128)(2,1)S(1)}, u32[]{:S(2)}, u32[]{:S(2)}) collective-permute-start(bf16[256,1024]{1,0:T(8,128)(2,1)S(1)} %add_convert_fusion.7), channel_id=1, source_target_pairs={{0,2},{1,3},{2,0},{3,1},{4,6},{5,7},{6,4},{7,5},{8,10},{9,11},{10,... | collective-permute-start | bytes 1572872 | tf_op jit(solution)/shard_map/ppermute | solution.py:576
  111.0 55.7 %collective-permute-start.11 = (bf16[256,1024]{1,0:T(8,128)(2,1)S(1)}, bf16[256,1024]{1,0:T(8,128)(2,1)S(1)}, u32[]{:S(2)}, u32[]{:S(2)}) collective-permute-start(bf16[256,1024]{1,0:T(8,128)(2,1)S(1)} %add_convert_fusion.4.mlp_own_ref), channel_id=1, source_target_pairs={{0,1},{1,0},{2,3},{3,2},{4,5},{5,4},{6,7},{7,6},{8,9},{9,8},{10,11... | collective-permute-start | bytes 1572872 | tf_op jit(solution)/shard_map/ppermute | solution.py:576
  111.1 53.4 %collective-permute-start.21 = (bf16[16,128,128]{2,1,0:T(8,128)(2,1)S(1)}, bf16[16,128,128]{2,1,0:T(8,128)(2,1)S(1)}, u32[]{:S(2)}, u32[]{:S(2)}) collective-permute-start(bf16[16,128,128]{2,1,0:T(8,128)(2,1)S(1)} %get-tuple-element.94), channel_id=1, source_target_pairs={{0,4},{4,0},{8,12},{12,8},{16,20},{20,16},{24,28},{28,24},{1,5},{5... | collective-permute-start | bytes 1572872 | tf_op jit(solution)/shard_map/ppermute | solution.py:576
  121.4 45.3 %collective-permute-start.8 = (bf16[256,1024]{1,0:T(8,128)(2,1)S(1)}, bf16[256,1024]{1,0:T(8,128)(2,1)S(1)}, u32[]{:S(2)}, u32[]{:S(2)}) collective-permute-start(bf16[256,1024]{1,0:T(8,128)(2,1)S(1)} %add_convert_fusion.6.normed_own_ref), channel_id=1, source_target_pairs={{0,1},{1,0},{2,3},{3,2},{4,5},{5,4},{6,7},{7,6},{8,9},{9,8},{10,11... | collective-permute-start | bytes 1572872 | tf_op jit(solution)/shard_map/ppermute | solution.py:576
  126.0 51.2 %collective-permute-start.16 = (bf16[20,128,128]{2,1,0:T(8,128)(2,1)S(1)}, bf16[20,128,128]{2,1,0:T(8,128)(2,1)S(1)}, u32[]{:S(2)}, u32[]{:S(2)}) collective-permute-start(bf16[20,128,128]{2,1,0:T(8,128)(2,1)S(1)} %get-tuple-element.121), channel_id=1, source_target_pairs={{0,8},{4,12},{8,0},{12,4},{16,24},{20,28},{24,16},{28,20},{1,9},{5... | collective-permute-start | bytes 1966088 | tf_op jit(solution)/shard_map/ppermute | solution.py:576
  154.1 26.0 %collective-permute-start.19 = (bf16[20,128,128]{2,1,0:T(8,128)(2,1)S(1)}, bf16[20,128,128]{2,1,0:T(8,128)(2,1)S(1)}, u32[]{:S(2)}, u32[]{:S(2)}) collective-permute-start(bf16[20,128,128]{2,1,0:T(8,128)(2,1)S(1)} %get-tuple-element.119), channel_id=1, source_target_pairs={{0,8},{4,12},{8,0},{12,4},{16,24},{20,28},{24,16},{28,20},{1,9},{5... | collective-permute-start | bytes 1966088 | tf_op jit(solution)/shard_map/ppermute | solution.py:576
  164.8 15.9 %collective-permute-start.22 = (bf16[8,128,128]{2,1,0:T(8,128)(2,1)S(1)}, bf16[8,128,128]{2,1,0:T(8,128)(2,1)S(1)}, u32[]{:S(2)}, u32[]{:S(2)}) collective-permute-start(bf16[8,128,128]{2,1,0:T(8,128)(2,1)S(1)} %get-tuple-element.127), channel_id=1, source_target_pairs={{0,8},{4,12},{8,0},{12,4},{16,24},{20,28},{24,16},{28,20},{1,9},{5... | collective-permute-start | bytes 786440 | tf_op jit(solution)/shard_map/ppermute | solution.py:576
  175.8 7.7 %collective-permute-start.12 = (f32[8,1024]{1,0:T(8,128)S(1)}, f32[8,1024]{1,0:T(8,128)S(1)}, u32[]{:S(2)}, u32[]{:S(2)}) collective-permute-start(f32[8,1024]{1,0:T(8,128)S(1)} %slice.78), channel_id=1, source_target_pairs={{0,4},{4,0},{8,12},{12,8},{16,20},{20,16},{24,28},{28,24},{1,5},{5... | collective-permute-start | bytes 98312 | tf_op jit(solution)/shard_map/ppermute | solution.py:576
  177.5 37.7 %collective-permute-start.17 = (bf16[10,128,128]{2,1,0:T(8,128)(2,1)S(1)}, bf16[10,128,128]{2,1,0:T(8,128)(2,1)S(1)}, u32[]{:S(2)}, u32[]{:S(2)}) collective-permute-start(bf16[10,128,128]{2,1,0:T(8,128)(2,1)S(1)} %get-tuple-element.124), channel_id=1, source_target_pairs={{0,16},{4,20},{8,24},{12,28},{16,0},{20,4},{24,8},{28,12},{1,17},{... | collective-permute-start | bytes 983048 | tf_op jit(solution)/shard_map/ppermute | solution.py:576
  180.3 34.8 %collective-permute-start.20 = (bf16[10,128,128]{2,1,0:T(8,128)(2,1)S(1)}, bf16[10,128,128]{2,1,0:T(8,128)(2,1)S(1)}, u32[]{:S(2)}, u32[]{:S(2)}) collective-permute-start(bf16[10,128,128]{2,1,0:T(8,128)(2,1)S(1)} %get-tuple-element.122), channel_id=1, source_target_pairs={{0,16},{4,20},{8,24},{12,28},{16,0},{20,4},{24,8},{28,12},{1,17},{... | collective-permute-start | bytes 983048 | tf_op jit(solution)/shard_map/ppermute | solution.py:576
  180.8 34.3 %collective-permute-start.23 = (bf16[4,128,128]{2,1,0:T(8,128)(2,1)S(1)}, bf16[4,128,128]{2,1,0:T(8,128)(2,1)S(1)}, u32[]{:S(2)}, u32[]{:S(2)}) collective-permute-start(bf16[4,128,128]{2,1,0:T(8,128)(2,1)S(1)} %get-tuple-element.128), channel_id=1, source_target_pairs={{0,16},{4,20},{8,24},{12,28},{16,0},{20,4},{24,8},{28,12},{1,17},{... | collective-permute-start | bytes 393224 | tf_op jit(solution)/shard_map/ppermute | solution.py:576
  183.5 13.8 %collective-permute-start.13 = (f32[8,1024]{1,0:T(8,128)S(1)}, f32[8,1024]{1,0:T(8,128)S(1)}, u32[]{:S(2)}, u32[]{:S(2)}) collective-permute-start(f32[8,1024]{1,0:T(8,128)S(1)} %slice_add_fusion), channel_id=1, source_target_pairs={{0,8},{4,12},{8,0},{12,4},{16,24},{20,28},{24,16},{28,20},{1,9},{5... | collective-permute-start | bytes 98312 | tf_op jit(solution)/shard_map/ppermute | solution.py:576
  197.3 17.8 %collective-permute-start.14 = (f32[8,1024]{1,0:T(8,128)S(1)}, f32[8,1024]{1,0:T(8,128)S(1)}, u32[]{:S(2)}, u32[]{:S(2)}) collective-permute-start(f32[8,1024]{1,0:T(8,128)S(1)} %add.93), channel_id=1, source_target_pairs={{0,16},{4,20},{8,24},{12,28},{16,0},{20,4},{24,8},{28,12},{1,17},{... | collective-permute-start | bytes 98312 | tf_op jit(solution)/shard_map/ppermute | solution.py:576
  220.2 3.6 %collective-permute-start.25 = (f32[8,128]{1,0:T(8,128)S(1)}, f32[8,128]{1,0:T(8,128)S(1)}, u32[]{:S(2)}, u32[]{:S(2)}) collective-permute-start(f32[8,128]{1,0:T(8,128)S(1)} %add.107), channel_id=1, source_target_pairs={{0,2},{1,3},{2,0},{3,1},{4,6},{5,7},{6,4},{7,5},{8,10},{9,11},{10,... | collective-permute-start | bytes 12296 | tf_op jit(solution)/shard_map/ppermute | solution.py:576
  231.0 4.5 %collective-permute-start.28 = (f32[8,128]{1,0:T(8,128)S(1)}, f32[8,128]{1,0:T(8,128)S(1)}, u32[]{:S(2)}, u32[]{:S(2)}) collective-permute-start(f32[8,128]{1,0:T(8,128)S(1)} %add.110), channel_id=1, source_target_pairs={{0,16},{4,20},{8,24},{12,28},{16,0},{20,4},{24,8},{28,12},{1,17},{... | collective-permute-start | bytes 12296 | tf_op jit(solution)/shard_map/ppermute | solution.py:576
  (33 other events, 348.0 us)
